TPU v7x, 32 devices: a whole 2x2x4 slice. The times are simulated.
32 devices in a mesh: shell: 4 (over z), sector: 8 (over y, x, core).
Axes of the slice: x: 2, y: 2, z: 4, core: 2. Of those that a mesh axis runs over, the one named last changes fastest.
Arguments:
- bricks: bfloat16 [4, 64, 32, 512], P('shell', 'sector'), may hold values from -6 to 6
- conv_w: bfloat16 [32, 864], replicated, may hold values from -0.21875 to 0.21875
- conv_b: float32 [32], replicated, may hold values from -3 to 3
- head_w1: bfloat16 [32, 64], replicated, may hold values from -1 to 1
- head_b1: float32 [64], replicated, may hold values from -3 to 3
- head_w2: float32 [64, 2], replicated, may hold values from -0.75 to 0.75
- queries: int32 [4, 64, 1024], P('shell', 'sector'), may hold values from -1 to 4095, as said below
- sample_src: int32 [4, 32768], P('shell', 'sector'), may hold values from 0 to 8191, as said below
- depth_target: float32 [4096], P('sector'), may hold values from 0.1 to 0.9
- inten_target: float32 [4096], P('sector'), may hold values from 0 to 1
- drop_label: int32 [4096], P('sector'), may hold values 0 or 1
Outputs:
- loss_mean: float32 [], replicated
- grad_conv_w: float32 [32, 864], replicated
- grad_conv_b: float32 [32], replicated
- grad_head_w1: float32 [32, 64], replicated
- grad_head_b1: float32 [64], replicated
- grad_head_w2: float32 [64, 2], replicated
- grad_bricks: bfloat16 [4, 64, 32, 512], P('shell', 'sector')
- ray_depth: float32 [4096], P('sector')
Inputs may be any that keep to these rules, and one draw needn't show every extreme that they name: `queries`: entry of the buffer from a device of sector v to owner w: a cell address (brick of the owner times 512 plus cell) or -1 for an empty slot. Every sample of a device holds exactly one live slot, named by sample_src as w * 1024 + slot. In every shell one owner receives full buffers of 1024 from every sector. `sample_src`: A slot w * 1024 + slot of the sample's own device; distinct samples of a device have distinct slots.
All inputs are finite; a program needn't handle non-finite values. No bound on the sum of `drop_label` on one device may be relied on, other than what follows from the above.
Results may differ from a plain program's by a relative error of at most 0.0015.
The roundings to bfloat16 on the way count: a program that leaves them out, or rounds other values in their place, can miss the bound.
Values may be sent and summed in bfloat16 or wider, within the bound.
A program may use at most 192 MiB of HBM per device.

v0:
```python
import functools
import math

import jax
import jax.numpy as jnp
from jax import lax
from jax.experimental import pallas as pl
from jax.experimental.pallas import tpu as pltpu
from jax.sharding import PartitionSpec as P

SAMP = 8
MESH = pl.DeviceIdType.MESH
F32 = jnp.float32
BF16 = jnp.bfloat16
GELU_SCALE = math.sqrt(2.0 / math.pi)
GELU_CUBIC = 0.044715
NT = (((1,), (1,)), ((), ()))


def gelu_and_slope(x):
    square = x * x
    t = jnp.tanh(GELU_SCALE * (x + GELU_CUBIC * (x * square)))
    half = 0.5 * (1.0 + t)
    slope = half + 0.5 * x * (1.0 - t * t) * (GELU_SCALE * (1.0 + 3.0 * GELU_CUBIC * square))
    return x * half, slope


def split(value, count):
    pieces = []
    for _ in range(count - 1):
        piece = value.astype(BF16).astype(F32)
        pieces.append(piece)
        value = value - piece
    return pieces + [value]


def matmul(a, b):
    return jnp.dot(a, b, preferred_element_type=F32)


def matmul_nt(a, b):
    return lax.dot_general(a, b, NT, preferred_element_type=F32)


def shifted(x, step, coord):
    width = x.shape[1]
    out = []
    for move in (-1, 0, 1):
        if move == 0:
            out.append(x)
        else:
            rolled = pltpu.roll(x, (-move * step) % width, 1)
            inside = coord >= 1 if move < 0 else coord <= 6
            out.append(rolled * jnp.where(inside, 1.0, 0.0))
    return out


def unfold(x, put):
    lane = lax.broadcasted_iota(jnp.int32, (1, x.shape[1]), 1)
    by_c = shifted(x, 1, lane & 7)
    for c in range(3):
        by_b = shifted(by_c[c], 8, (lane >> 3) & 7)
        for b in range(3):
            by_a = shifted(by_b[b], 64, lane >> 6)
            for a in range(3):
                put(9 * a + 3 * b + c, by_a[a].astype(BF16))


def body(
    shells,
    sectors,
    bricks,
    conv_w,
    conv_back_w,
    conv_b,
    w1_t,
    w1_rep,
    b1,
    w2,
    queries,
    sources,
    depth_target,
    inten_target,
    drop_label,
    grad_bricks,
    ray_depth_out,
    reduced,
    addr,
    decoded,
    slope_conv,
    cols,
    addr_hot,
    src_hot,
    rep_send,
    rep_recv,
    hid_val,
    hid_slope,
    dens_slot,
    inten_slot,
    gd_slot,
    gi_slot,
    shell_buf,
    grad_send,
    grad_recv,
    cell_grad,
    pack,
    red_recv,
    wgrad,
    w1_acc,
    small_acc,
    req_sems,
    rep_sems,
    shell_sems,
    grad_sems,
    red_sems,
    out_sems,
    own_sem,
):
    n = sectors
    count = shells * sectors
    nb, ch, cells = bricks.shape
    cap = queries.shape[2]
    hid = w1_t.shape[0]
    rays = sources.shape[2]
    shift = cap.bit_length() - 1
    shell = lax.axis_index("shell")
    sector = lax.axis_index("sector")
    me = shell * n + sector

    def flat_peer(k):
        peer = lax.rem(me + k, count)
        return peer, {"shell": lax.div(peer, n), "sector": lax.rem(peer, n)}

    barrier = pltpu.get_barrier_semaphore()

    @pl.loop(1, count)
    def _(k):
        _, where = flat_peer(k)
        pl.semaphore_signal(barrier, inc=1, device_id=where, device_id_type=MESH)

    pl.semaphore_wait(barrier, count - 1)

    def to_sector(src, dst, sems, k):
        peer = lax.rem(sector + k, n)
        return pltpu.make_async_remote_copy(
            src_ref=src.at[peer],
            dst_ref=dst.at[sector],
            send_sem=sems.at[0, k],
            recv_sem=sems.at[1, k],
            device_id={"shell": shell, "sector": peer},
            device_id_type=MESH,
        )

    @pl.loop(1, n)
    def _(k):
        to_sector(queries, addr, req_sems, k).start()

    own = pltpu.make_async_copy(queries.at[sector], addr.at[sector], own_sem)
    own.start()

    @pl.loop(0, nb)
    def _(b):
        def put(k, value):
            cols[pl.ds(k * ch, ch), :] = value

        unfold(bricks[b].astype(F32), put)
        pre = matmul(conv_w[...], cols[...]) + conv_b[...]
        value, slope = gelu_and_slope(pre)
        decoded[pl.ds(pl.multiple_of(b * ch, ch), ch), :] = value.astype(BF16)
        slope_conv[pl.ds(pl.multiple_of(b * ch, ch), ch), :] = slope

    own.wait()

    @pl.loop(1, n)
    def _(k):
        to_sector(queries, addr, req_sems, k).wait()

    def gather_for(v, out_ref):
        where = addr[v]
        cell = where & (cells - 1)
        brick = jnp.broadcast_to(where >> (cells.bit_length() - 1), (ch, cap))
        rows = lax.broadcasted_iota(jnp.int32, (cells, cap), 0)
        addr_hot[v] = jnp.where(rows == cell, 1.0, 0.0).astype(BF16)
        picked = matmul(decoded[...], addr_hot[v])
        feats = jnp.zeros((ch, cap), F32)
        for b in range(nb):
            feats = feats + jnp.where(brick == b, picked[b * ch : (b + 1) * ch], 0.0)
        out_ref[v] = feats.astype(BF16)

    @pl.loop(1, n)
    def _(k):
        gather_for(lax.rem(sector + k, n), rep_send)
        to_sector(rep_send, rep_recv, rep_sems, k).start()

    gather_for(sector, rep_recv)

    @pl.loop(0, SAMP)
    def _(k):
        rows = lax.broadcasted_iota(jnp.int32, (cap, rays), 0)
        src_hot[k] = jnp.where(rows == (sources[k] & (cap - 1)), 1.0, 0.0).astype(BF16)

    def head_for(w):
        feats = rep_recv[w]
        value, slope = gelu_and_slope(matmul(w1_t[...], feats) + b1[...])
        hid_val[w] = value
        hid_slope[w] = slope
        dens_slot[pl.ds(w, 1), :] = jnp.sum(value * w2[:, 0:1], axis=0, keepdims=True)
        inten_slot[pl.ds(w, 1), :] = jnp.sum(value * w2[:, 1:2], axis=0, keepdims=True)

    head_for(sector)

    @pl.loop(1, n)
    def _(k):
        to_sector(rep_send, rep_recv, rep_sems, k).wait()
        head_for(lax.rem(sector + n - k, n))

    e0 = dens_slot[...]
    e1 = inten_slot[...]
    dens_all = jnp.maximum(e0, 0.0) + jnp.log1p(jnp.exp(-jnp.abs(e0)))
    inten_all = 1.0 / (1.0 + jnp.exp(-e1))
    slots = jnp.concatenate([dens_all, inten_all], axis=0)
    slot_pieces = jnp.concatenate([p.astype(BF16) for p in split(slots, 3)], axis=0)
    owner_rows = lax.broadcasted_iota(jnp.int32, (n, rays), 0)
    dens = []
    inten = []
    for k in range(SAMP):
        got = matmul(slot_pieces, src_hot[k])
        got = got[: 2 * n] + got[2 * n : 4 * n] + got[4 * n :]
        mine = owner_rows == (sources[k] >> shift)
        dens.append(jnp.sum(jnp.where(mine, got[:n], 0.0), axis=0, keepdims=True))
        inten.append(jnp.sum(jnp.where(mine, got[n:], 0.0), axis=0, keepdims=True))

    step_size = 2.0 / (shells * SAMP)
    span = 1.0 / (shells * SAMP)
    first = shell.astype(F32) * SAMP + 0.5
    before = jnp.zeros((1, rays), F32)
    depth = jnp.zeros((1, rays), F32)
    light = jnp.zeros((1, rays), F32)
    enter = []
    leave = []
    weight = []
    for k in range(SAMP):
        optical = dens[k] * step_size
        enter.append(jnp.exp(-before))
        leave.append(jnp.exp(-optical))
        weight.append(enter[k] * (1.0 - leave[k]))
        depth = depth + weight[k] * ((first + k) * span)
        light = light + weight[k] * inten[k]
        before = before + optical
    shell_buf[shell] = jnp.concatenate(
        [depth, light, before, jnp.zeros((5, rays), F32)], axis=0
    )

    def to_shell(k):
        return pltpu.make_async_remote_copy(
            src_ref=shell_buf.at[shell],
            dst_ref=shell_buf.at[shell],
            send_sem=shell_sems.at[0, k],
            recv_sem=shell_sems.at[1, k],
            device_id={"shell": lax.rem(shell + k, shells), "sector": sector},
            device_id_type=MESH,
        )

    for k in range(1, shells):
        to_shell(k).start()
    for k in range(1, shells):
        to_shell(k).wait()

    prefix = jnp.zeros((1, rays), F32)
    ray_depth = jnp.zeros((1, rays), F32)
    ray_light = jnp.zeros((1, rays), F32)
    entry = []
    for s in range(shells):
        entry.append(jnp.exp(-prefix))
        ray_depth = ray_depth + entry[s] * shell_buf[s, 0:1, :]
        ray_light = ray_light + entry[s] * shell_buf[s, 1:2, :]
        prefix = prefix + shell_buf[s, 2:3, :]
    ray_depth_out[...] = ray_depth
    escape = jnp.exp(-prefix)
    dropped = drop_label[...].astype(F32)
    kept = 1.0 - dropped
    off_depth = ray_depth - depth_target[...]
    off_light = ray_light - inten_target[...]
    off_escape = escape - dropped
    loss = jnp.sum(
        kept * (off_depth * off_depth + off_light * off_light) + off_escape * off_escape,
        axis=1,
        keepdims=True,
    )
    grad_depth = 2.0 * kept * off_depth
    grad_light = 2.0 * kept * off_light
    behind = jnp.zeros((1, rays), F32)
    own_entry = jnp.zeros((1, rays), F32)
    for s in range(shells):
        term = (grad_depth * shell_buf[s, 0:1, :] + grad_light * shell_buf[s, 1:2, :]) * entry[s]
        behind = behind + jnp.where(shell < s, term, 0.0)
        own_entry = own_entry + jnp.where(shell == s, entry[s], 0.0)
    cot_depth = grad_depth * own_entry
    cot_light = grad_light * own_entry
    cot_tau = -2.0 * off_escape * escape - behind
    later = jnp.zeros((1, rays), F32)
    dens_grad = [None] * SAMP
    inten_grad = [None] * SAMP
    for k in reversed(range(SAMP)):
        pull = cot_depth * ((first + k) * span) + cot_light * inten[k]
        inten_grad[k] = cot_light * weight[k]
        dens_grad[k] = step_size * (pull * enter[k] * leave[k] - later + cot_tau)
        later = later + pull * weight[k]
    slot_grad = jnp.zeros((6 * n, cap), F32)
    for k in range(SAMP):
        mine = owner_rows == (sources[k] >> shift)
        both = jnp.concatenate(
            [jnp.where(mine, dens_grad[k], 0.0), jnp.where(mine, inten_grad[k], 0.0)], axis=0
        )
        both = jnp.concatenate([p.astype(BF16) for p in split(both, 3)], axis=0)
        slot_grad = slot_grad + matmul_nt(both, src_hot[k])
    slot_grad = slot_grad[: 2 * n] + slot_grad[2 * n : 4 * n] + slot_grad[4 * n :]
    gd_slot[...] = slot_grad[:n] * (1.0 / (1.0 + jnp.exp(-e0)))
    gi_slot[...] = slot_grad[n:] * (inten_all * (1.0 - inten_all))

    w1_acc[...] = jnp.zeros_like(w1_acc)
    small_acc[...] = jnp.zeros_like(small_acc)

    def head_back(w, out_ref, at):
        g0 = gd_slot[pl.ds(w, 1), :]
        g1 = gi_slot[pl.ds(w, 1), :]
        value = hid_val[w]
        grad = (w2[:, 0:1] * g0 + w2[:, 1:2] * g1) * hid_slope[w]
        pieces = jnp.concatenate([p.astype(BF16) for p in split(grad, 3)], axis=0)
        out_ref[at] = matmul(w1_rep[...], pieces)
        w1_acc[...] += matmul_nt(rep_recv[w], pieces)
        small_acc[0] += jnp.sum(grad, axis=1, keepdims=True)
        small_acc[1] += jnp.sum(value * g0, axis=1, keepdims=True)
        small_acc[2] += jnp.sum(value * g1, axis=1, keepdims=True)

    @pl.loop(1, n)
    def _(k):
        w = lax.rem(sector + k, n)
        head_back(w, grad_send, w)
        to_sector(grad_send, grad_recv, grad_sems, k).start()

    head_back(sector, grad_recv, sector)

    cell_grad[...] = jnp.zeros_like(cell_grad)

    def scatter_from(v):
        brick = jnp.broadcast_to(addr[v] >> (cells.bit_length() - 1), (ch, cap))
        high, low = split(grad_recv[v], 2)
        spread = jnp.concatenate(
            [jnp.where(brick == b, p, 0.0).astype(BF16) for p in (high, low) for b in range(nb)],
            axis=0,
        )
        added = matmul_nt(spread, addr_hot[v])
        cell_grad[...] += added[: nb * ch] + added[nb * ch :]

    scatter_from(sector)

    @pl.loop(1, n)
    def _(k):
        to_sector(grad_send, grad_recv, grad_sems, k).wait()
        scatter_from(lax.rem(sector + n - k, n))

    wgrad[...] = jnp.zeros_like(wgrad)
    wide = wgrad.shape[1]
    used = 27 * ch

    def conv_back(b, bias):
        def put(k, value):
            cols[pl.ds(k * ch, ch), :] = value

        at = pl.ds(pl.multiple_of(b * ch, ch), ch)
        cot = (cell_grad[at, :] * slope_conv[at, :]).astype(BF16)
        unfold(cot.astype(F32), put)
        grad_bricks[b] = matmul(conv_back_w[...], cols[...]).astype(BF16)
        wgrad[:, :used] += matmul_nt(bricks[b], cols[...])
        return bias + jnp.sum(cot.astype(F32), axis=1, keepdims=True)

    bias_grad = lax.fori_loop(0, nb, conv_back, jnp.zeros((ch, 1), F32))

    tiles = wide // 128
    for t in range(tiles):
        for part in range(ch // 8):
            pack[t * (ch // 8) + part] = wgrad[part * 8 : part * 8 + 8, t * 128 : t * 128 + 128]
    lane = lax.broadcasted_iota(jnp.int32, (ch, 128), 1)
    w1_all = w1_acc[...]
    w1_grad = w1_all[:, :hid] + w1_all[:, hid : 2 * hid] + w1_all[:, 2 * hid :]
    last = jnp.concatenate([w1_grad, jnp.zeros((ch, 128 - hid), F32)], axis=1)
    place = hid
    for j in range(3):
        for part in range(hid // ch):
            column = small_acc[j, part * ch : (part + 1) * ch, :]
            last = last + jnp.where(lane == place, column, 0.0)
            place += 1
    last = last + jnp.where(lane == place, bias_grad, 0.0)
    loss_here = jnp.where(shell == 0, loss, 0.0)
    last = last + jnp.where(lane == place + 1, loss_here, 0.0)
    base = tiles * (ch // 8)
    for part in range(ch // 8):
        pack[base + part] = last[part * 8 : part * 8 + 8]
    for extra in range(base + ch // 8, pack.shape[0]):
        pack[extra] = jnp.zeros((8, 128), F32)

    def to_reducer(k):
        peer, where = flat_peer(k)
        return pltpu.make_async_remote_copy(
            src_ref=pack.at[peer],
            dst_ref=red_recv.at[me],
            send_sem=red_sems.at[0, k],
            recv_sem=red_sems.at[1, k],
            device_id=where,
            device_id_type=MESH,
        )

    def to_everyone(k):
        _, where = flat_peer(k)
        return pltpu.make_async_remote_copy(
            src_ref=reduced.at[me],
            dst_ref=reduced.at[me],
            send_sem=out_sems.at[0, k],
            recv_sem=out_sems.at[1, k],
            device_id=where,
            device_id_type=MESH,
        )

    @pl.loop(1, count)
    def _(k):
        to_reducer(k).start()

    red_recv[me] = pack[me]

    @pl.loop(1, count)
    def _(k):
        to_reducer(k).wait()

    reduced[me] = jnp.sum(red_recv[...], axis=0)

    @pl.loop(1, count)
    def _(k):
        to_everyone(k).start()

    @pl.loop(1, count)
    def _(k):
        to_everyone(k).wait()


def local(
    bricks,
    conv_w,
    conv_b,
    head_w1,
    head_b1,
    head_w2,
    queries,
    sample_src,
    depth_target,
    inten_target,
    drop_label,
):
    shells = lax.axis_size("shell")
    n = lax.axis_size("sector")
    count = shells * n
    _, nb, ch, cells = bricks.shape
    cap = queries.shape[2]
    hid = head_w1.shape[1]
    rays = depth_target.shape[0]
    wide = -(-27 * ch // 128) * 128
    chunks = (wide // 128 + 1) * (ch // 8)
    held = max(count, -(-chunks // count) * count)
    assert held == count and cap & (cap - 1) == 0 and cells == 512
    conv_back_w = conv_w.reshape(ch, 27, ch)[:, ::-1].transpose(2, 1, 0).reshape(ch, 27 * ch)
    operands = (
        bricks[0],
        conv_w,
        conv_back_w,
        conv_b[:, None],
        head_w1.T,
        jnp.concatenate([head_w1] * 3, axis=1),
        head_b1[:, None],
        head_w2,
        queries[0][:, None, :],
        sample_src[0].reshape(rays, SAMP).T[:, None, :],
        depth_target[None],
        inten_target[None],
        drop_label[None],
    )
    vmem = pl.BlockSpec(memory_space=pltpu.VMEM)
    dma = pltpu.SemaphoreType.DMA
    grad_bricks, ray_depth, reduced = pl.pallas_call(
        functools.partial(body, shells, n),
        out_shape=(
            jax.ShapeDtypeStruct((nb, ch, cells), BF16),
            jax.ShapeDtypeStruct((1, rays), F32),
            jax.ShapeDtypeStruct((held, 8, 128), F32),
        ),
        in_specs=[vmem] * len(operands),
        out_specs=(vmem, vmem, vmem),
        scratch_shapes=[
            pltpu.VMEM((n, 1, cap), jnp.int32),
            pltpu.VMEM((nb * ch, cells), BF16),
            pltpu.VMEM((nb * ch, cells), F32),
            pltpu.VMEM((27 * ch, cells), BF16),
            pltpu.VMEM((n, cells, cap), BF16),
            pltpu.VMEM((SAMP, cap, rays), BF16),
            pltpu.VMEM((n, ch, cap), BF16),
            pltpu.VMEM((n, ch, cap), BF16),
            pltpu.VMEM((n, hid, cap), F32),
            pltpu.VMEM((n, hid, cap), F32),
            pltpu.VMEM((n, cap), F32),
            pltpu.VMEM((n, cap), F32),
            pltpu.VMEM((n, cap), F32),
            pltpu.VMEM((n, cap), F32),
            pltpu.VMEM((shells, 8, rays), F32),
            pltpu.VMEM((n, ch, cap), F32),
            pltpu.VMEM((n, ch, cap), F32),
            pltpu.VMEM((nb * ch, cells), F32),
            pltpu.VMEM((held, 8, 128), F32),
            pltpu.VMEM((count, 8, 128), F32),
            pltpu.VMEM((ch, wide), F32),
            pltpu.VMEM((ch, 3 * hid), F32),
            pltpu.VMEM((3, hid, 1), F32),
            dma((2, n)),
            dma((2, n)),
            dma((2, shells)),
            dma((2, n)),
            dma((2, count)),
            dma((2, count)),
            dma,
        ],
        compiler_params=pltpu.CompilerParams(
            collective_id=0, has_side_effects=True, vmem_limit_bytes=56 * 1024 * 1024
        ),
    )(*operands)
    tiles = wide // 128
    flat = reduced.reshape(-1, 128)
    conv_grad = flat[: tiles * ch].reshape(tiles, ch, 128).transpose(1, 0, 2).reshape(ch, wide)
    conv_grad = conv_grad[:, : 27 * ch].reshape(ch, 27, ch)[:, ::-1].transpose(2, 1, 0)
    last = flat[tiles * ch : (tiles + 1) * ch]
    per = hid // ch
    columns = last[:, hid : hid + 3 * per].T.reshape(3, hid)
    place = hid + 3 * per
    return (
        last[0, place + 1] / (rays * n),
        conv_grad.reshape(ch, 27 * ch),
        last[:, place],
        last[:, :hid],
        columns[0],
        columns[1:].T,
        grad_bricks[None],
        ray_depth[0],
    )


def solution(mesh):
    return jax.shard_map(
        local,
        mesh=mesh,
        in_specs=(
            P("shell", "sector", None, None),
            P(),
            P(),
            P(),
            P(),
            P(),
            P("shell", "sector", None),
            P("shell", "sector"),
            P("sector"),
            P("sector"),
            P("sector"),
        ),
        out_specs=(P(), P(), P(), P(), P(), P(), P("shell", "sector", None, None), P("sector")),
        check_vma=False,
    )
```

profile of v0, /device:TPU:0, one launch (start us, length us, event | category | flops | bytes accessed | tf_op | source)
XLA Modules:
  0.0 85.0 jit_solution(1407448975193661638)
XLA Ops:
  0.6 1.0 %reshape.44 = bf16[32,27,32]{2,1,0:T(8,128)(2,1)S(1)} reshape(bf16[32,864]{1,0:T(8,128)(2,1)} %conv_w.1) | data formatting | bytes 110592 | tf_op jit(solution)/shard_map/reshape | solution.py:470
  1.7 0.2 rev.6
  1.9 0.6 copy.26
  2.4 0.9 %reshape.45.conv_back_w = bf16[32,864]{1,0:T(8,128)(2,1)} reshape(bf16[32,27,32]{2,1,0:T(8,128)(2,1)S(1)} %copy.26) | data formatting | bytes 110592 | tf_op jit(solution)/shard_map/reshape | solution.py:470
  3.3 0.7 copy-done.8
  4.0 0.7 copy.29.conv_b
  4.7 0.7 copy.27
  5.4 0.7 pad_maximum_fusion.w1_rep
  6.0 0.7 copy-done.7
  6.7 0.7 copy.30.b1
  7.4 0.7 copy.31.w2
  8.1 0.6 broadcast_in_dim_squeeze.3.queries
  8.7 0.5 broadcast.4
  9.3 0.7 reduce.5
  9.9 0.2 reshape_squeeze.3
  10.1 0.1 copy.28
  10.2 0.6 broadcast_in_dim.23.sources
  10.8 64.8 %shard_map.170 = (bf16[8,32,512]{2,1,0:T(8,128)(2,1)}, f32[1,512]{1,0:T(1,128)}, f32[32,8,128]{2,1,0:T(8,128)}) custom-call(bf16[8,32,512]{2,1,0:T(8,128)(2,1)} %bitcast.32, bf16[32,864]{1,0:T(8,128)(2,1)} %conv_w.1, bf16[32,864]{1,0:T(8,128)(2,1)} %reshape.45.conv_back_w, f32[32,1]{1,0:T(8,128)} %copy.29.conv_b, bf16[64,32]{1,0:T(8,128)(2,1)} %bitcast.36, ...), custom_call_target="tpu_custom_call" | custom-call | tf_op jit(solution)/shard_map/pallas_call | solution.py:488
  75.6 0.7 slice_bitcast_fusion.1
  76.4 0.6 slice.46
  77.6 0.9 %slice.38 = f32[28,8,128]{2,1,0:T(8,128)S(1)} slice(f32[32,8,128]{2,1,0:T(8,128)} %get-tuple-element.11), slice={[0:28], [0:8], [0:128]} | slice | bytes 229376 | tf_op jit(solution)/shard_map/slice | solution.py:535
  78.6 0.2 reshape.48
  78.8 0.2 rev.7
  79.0 0.6 copy.33
  79.5 0.8 reshape.49
  80.4 0.7 slice_reduce_fusion
  81.1 0.1 copy.34
  81.2 0.6 squeeze.15
  81.9 0.1 copy.35
  82.0 0.7 slice.45
  82.6 0.7 copy.41
  83.3 0.6 copy.42
  (20 shorter events, 0.3 us)
Async XLA Ops:
  3.3 0.7 copy-start.8
  4.0 0.7 copy-start.2
  5.4 2.1 %copy-start.6 = (f32[64,2]{0,1:T(2,128)S(1)}, f32[64,2]{0,1:T(2,128)}, u32[]{:S(2)}) copy-start(f32[64,2]{0,1:T(2,128)} %param.16) | copy-start | bytes 1540
  6.0 0.7 copy-start.7
  6.7 1.4 %copy-start.3 = (s32[1,8,1024]{2,1,0:T(8,128)S(1)}, s32[1,8,1024]{2,1,0:T(8,128)}, u32[]{:S(2)}) copy-start(s32[1,8,1024]{2,1,0:T(8,128)} %param.17) | copy-start | bytes 98308
  8.1 1.1 %copy-start.4 = (s32[1,4096]{1,0:T(1,128)S(1)}, s32[1,4096]{1,0:T(1,128)}, u32[]{:S(2)}) copy-start(s32[1,4096]{1,0:T(1,128)} %param.18) | copy-start | bytes 49156
  76.4 4.7 %copy-start.1 = (f32[32,128]{1,0:T(8,128)}, f32[32,128]{1,0:T(8,128)S(1)}, u32[]{:S(2)}) copy-start(f32[32,128]{1,0:T(8,128)S(1)} %slice_bitcast_fusion.1) | copy-start | bytes 49156
  79.5 3.1 %copy-start = (bf16[8,32,512]{2,1,0:T(8,128)(2,1)S(1)}, bf16[8,32,512]{2,1,0:T(8,128)(2,1)}, u32[]{:S(2)}) copy-start(bf16[8,32,512]{2,1,0:T(8,128)(2,1)} %get-tuple-element.12) | copy-start | bytes 786436
  82.6 0.7 copy-start.5
where the time goes:
time: 85.4 us; the launch traced here: 85 us
  Pallas kernels  64.8 us (76%)
  local copies, waits for them, and re-layouts  16.4 us (19%)
  between operations  2.52 us (3%)
  other arithmetic  1.37 us (2%)
    pallas_call x1, Pallas kernels, local(): pl.pallas_call(functools.partial(body, shells, n), out_shape=(jax.ShapeDt...  64.8 us
    unnamed x24, local copies, waits for them, and re-layouts  4.54 us
    reshape x2, local copies, waits for them, and re-layouts, local(): conv_w.reshape(ch, 27, ch)[:, ::-1].transpose(2, 1, 0).reshape(ch, 27 * ch)  1.9 us

commit v1 on v0

--- a/solution.py
+++ b/solution.py
@@ -66,29 +66,47 @@
                 put(9 * a + 3 * b + c, by_a[a].astype(BF16))
 
 
+def column(row):
+    size = row.shape[1]
+    i = lax.broadcasted_iota(jnp.int32, (size, size), 0)
+    j = lax.broadcasted_iota(jnp.int32, (size, size), 1)
+    return jnp.sum(jnp.where(i == j, row, 0.0), axis=1, keepdims=True)
+
+
+def repeated_eye(size, times):
+    i = lax.broadcasted_iota(jnp.int32, (size, size), 0)
+    j = lax.broadcasted_iota(jnp.int32, (size, size), 1)
+    eye = jnp.where(i == j, 1.0, 0.0)
+    return jnp.concatenate([eye] * times, axis=1).astype(BF16)
+
+
 def body(
     shells,
     sectors,
     bricks,
     conv_w,
-    conv_back_w,
     conv_b,
-    w1_t,
-    w1_rep,
+    w1,
     b1,
     w2,
     queries,
-    sources,
+    sample_src,
     depth_target,
     inten_target,
     drop_label,
     grad_bricks,
     ray_depth_out,
     reduced,
+    conv_back_w,
+    w1_t,
+    w1_rep,
+    sources,
+    asked,
     addr,
     decoded,
     slope_conv,
     cols,
+    cot_cols,
     addr_hot,
     src_hot,
     rep_send,
@@ -105,9 +123,6 @@
     cell_grad,
     pack,
     red_recv,
-    wgrad,
-    w1_acc,
-    small_acc,
     req_sems,
     rep_sems,
     shell_sems,
@@ -119,9 +134,9 @@
     n = sectors
     count = shells * sectors
     nb, ch, cells = bricks.shape
-    cap = queries.shape[2]
-    hid = w1_t.shape[0]
-    rays = sources.shape[2]
+    cap = queries.shape[1]
+    hid = w1.shape[1]
+    rays = sources.shape[1]
     shift = cap.bit_length() - 1
     shell = lax.axis_index("shell")
     sector = lax.axis_index("sector")
@@ -138,81 +153,113 @@
         _, where = flat_peer(k)
         pl.semaphore_signal(barrier, inc=1, device_id=where, device_id_type=MESH)
 
+    for j in range(n):
+        asked[j] = queries[j : j + 1, :]
+    conv_b_col = column(conv_b[...])
+    b1_col = column(b1[...])
+    w2_density = column(w2[0:1, :])
+    w2_intensity = column(w2[1:2, :])
+    w1_t[...] = matmul_nt(repeated_eye(hid, 1), w1[...]).astype(BF16)
+    w1_rep[...] = matmul(w1[...], repeated_eye(hid, 3)).astype(BF16)
+    turned = jnp.transpose(conv_w[...].astype(F32))
+    conv_back_w[...] = jnp.concatenate(
+        [turned[k * ch : (k + 1) * ch] for k in reversed(range(27))], axis=1
+    ).astype(BF16)
+    block = SAMP * 128
+    ray_of = lax.broadcasted_iota(jnp.int32, (block, 128), 0) // SAMP
+    to_ray = jnp.where(ray_of == lax.broadcasted_iota(jnp.int32, (block, 128), 1), 1.0, 0.0)
+    to_ray = to_ray.astype(BF16)
+    sample_of = lax.broadcasted_iota(jnp.int32, (SAMP, block), 1) & (SAMP - 1)
+    own_row = sample_of == lax.broadcasted_iota(jnp.int32, (SAMP, block), 0)
+    for j in range(rays // 128):
+        part = sample_src[:, j * block : (j + 1) * block]
+        pair = [(part >> 7).astype(F32), (part & 127).astype(F32)]
+        pair = jnp.concatenate([jnp.where(own_row, p, 0.0) for p in pair], axis=0)
+        got = matmul(pair.astype(BF16), to_ray)
+        whole = got[:SAMP] * 128.0 + got[SAMP:]
+        sources[:, j * 128 : (j + 1) * 128] = whole.astype(jnp.int32)
+
     pl.semaphore_wait(barrier, count - 1)
 
-    def to_sector(src, dst, sems, k):
-        peer = lax.rem(sector + k, n)
+    def to_owner(src, dst, sems, k):
         return pltpu.make_async_remote_copy(
-            src_ref=src.at[peer],
-            dst_ref=dst.at[sector],
+            src_ref=src,
+            dst_ref=dst.at[k],
             send_sem=sems.at[0, k],
             recv_sem=sems.at[1, k],
-            device_id={"shell": shell, "sector": peer},
+            device_id={"shell": shell, "sector": lax.rem(sector + k, n)},
             device_id_type=MESH,
         )
 
-    @pl.loop(1, n)
-    def _(k):
-        to_sector(queries, addr, req_sems, k).start()
-
-    own = pltpu.make_async_copy(queries.at[sector], addr.at[sector], own_sem)
+    def to_asker(src, dst, sems, k):
+        return pltpu.make_async_remote_copy(
+            src_ref=src,
+            dst_ref=dst.at[k],
+            send_sem=sems.at[0, k],
+            recv_sem=sems.at[1, k],
+            device_id={"shell": shell, "sector": lax.rem(sector + n - k, n)},
+            device_id_type=MESH,
+        )
+
+    def request(k):
+        return to_owner(asked.at[lax.rem(sector + k, n)], addr, req_sems, k)
+
+    def reply(k):
+        return to_asker(rep_send.at[k], rep_recv, rep_sems, k)
+
+    def give_back(k):
+        return to_owner(grad_send.at[k], grad_recv, grad_sems, k)
+
+    for k in range(1, n):
+        request(k).start()
+
+    own = pltpu.make_async_copy(asked.at[sector], addr.at[0], own_sem)
     own.start()
 
-    @pl.loop(0, nb)
-    def _(b):
-        def put(k, value):
-            cols[pl.ds(k * ch, ch), :] = value
+    for b in range(nb):
+
+        def put(k, value, b=b):
+            cols[b, k * ch : (k + 1) * ch, :] = value
 
         unfold(bricks[b].astype(F32), put)
-        pre = matmul(conv_w[...], cols[...]) + conv_b[...]
-        value, slope = gelu_and_slope(pre)
-        decoded[pl.ds(pl.multiple_of(b * ch, ch), ch), :] = value.astype(BF16)
-        slope_conv[pl.ds(pl.multiple_of(b * ch, ch), ch), :] = slope
+        value, slope = gelu_and_slope(matmul(conv_w[...], cols[b]) + conv_b_col)
+        decoded[b * ch : (b + 1) * ch, :] = value.astype(BF16)
+        slope_conv[b * ch : (b + 1) * ch, :] = slope
 
     own.wait()
-
-    @pl.loop(1, n)
-    def _(k):
-        to_sector(queries, addr, req_sems, k).wait()
-
-    def gather_for(v, out_ref):
-        where = addr[v]
+    for k in range(1, n):
+        request(k).wait()
+
+    def gather_for(k, out_ref):
+        where = addr[k]
         cell = where & (cells - 1)
         brick = jnp.broadcast_to(where >> (cells.bit_length() - 1), (ch, cap))
         rows = lax.broadcasted_iota(jnp.int32, (cells, cap), 0)
-        addr_hot[v] = jnp.where(rows == cell, 1.0, 0.0).astype(BF16)
-        picked = matmul(decoded[...], addr_hot[v])
+        addr_hot[k] = jnp.where(rows == cell, 1.0, 0.0).astype(BF16)
+        picked = matmul(decoded[...], addr_hot[k])
         feats = jnp.zeros((ch, cap), F32)
         for b in range(nb):
             feats = feats + jnp.where(brick == b, picked[b * ch : (b + 1) * ch], 0.0)
-        out_ref[v] = feats.astype(BF16)
-
-    @pl.loop(1, n)
-    def _(k):
-        gather_for(lax.rem(sector + k, n), rep_send)
-        to_sector(rep_send, rep_recv, rep_sems, k).start()
-
-    gather_for(sector, rep_recv)
-
-    @pl.loop(0, SAMP)
-    def _(k):
+        out_ref[k] = feats.astype(BF16)
+
+    for k in range(1, n):
+        gather_for(k, rep_send)
+        reply(k).start()
+    gather_for(0, rep_recv)
+
+    for k in range(SAMP):
         rows = lax.broadcasted_iota(jnp.int32, (cap, rays), 0)
-        src_hot[k] = jnp.where(rows == (sources[k] & (cap - 1)), 1.0, 0.0).astype(BF16)
-
-    def head_for(w):
-        feats = rep_recv[w]
-        value, slope = gelu_and_slope(matmul(w1_t[...], feats) + b1[...])
-        hid_val[w] = value
-        hid_slope[w] = slope
-        dens_slot[pl.ds(w, 1), :] = jnp.sum(value * w2[:, 0:1], axis=0, keepdims=True)
-        inten_slot[pl.ds(w, 1), :] = jnp.sum(value * w2[:, 1:2], axis=0, keepdims=True)
-
-    head_for(sector)
-
-    @pl.loop(1, n)
-    def _(k):
-        to_sector(rep_send, rep_recv, rep_sems, k).wait()
-        head_for(lax.rem(sector + n - k, n))
+        slot = sources[k : k + 1, :] & (cap - 1)
+        src_hot[k] = jnp.where(rows == slot, 1.0, 0.0).astype(BF16)
+
+    for k in range(n):
+        if k > 0:
+            reply(k).wait()
+        value, slope = gelu_and_slope(matmul(w1_t[...], rep_recv[k]) + b1_col)
+        hid_val[k] = value
+        hid_slope[k] = slope
+        dens_slot[k : k + 1, :] = jnp.sum(value * w2_density, axis=0, keepdims=True)
+        inten_slot[k : k + 1, :] = jnp.sum(value * w2_intensity, axis=0, keepdims=True)
 
     e0 = dens_slot[...]
     e1 = inten_slot[...]
@@ -221,12 +268,14 @@
     slots = jnp.concatenate([dens_all, inten_all], axis=0)
     slot_pieces = jnp.concatenate([p.astype(BF16) for p in split(slots, 3)], axis=0)
     owner_rows = lax.broadcasted_iota(jnp.int32, (n, rays), 0)
+    owner_of = (sources[...] >> shift) - sector
+    owner_of = jnp.where(owner_of < 0, owner_of + n, owner_of)
     dens = []
     inten = []
     for k in range(SAMP):
         got = matmul(slot_pieces, src_hot[k])
         got = got[: 2 * n] + got[2 * n : 4 * n] + got[4 * n :]
-        mine = owner_rows == (sources[k] >> shift)
+        mine = owner_rows == owner_of[k : k + 1, :]
         dens.append(jnp.sum(jnp.where(mine, got[:n], 0.0), axis=0, keepdims=True))
         inten.append(jnp.sum(jnp.where(mine, got[n:], 0.0), axis=0, keepdims=True))
 
@@ -308,7 +357,7 @@
         later = later + pull * weight[k]
     slot_grad = jnp.zeros((6 * n, cap), F32)
     for k in range(SAMP):
-        mine = owner_rows == (sources[k] >> shift)
+        mine = owner_rows == owner_of[k : k + 1, :]
         both = jnp.concatenate(
             [jnp.where(mine, dens_grad[k], 0.0), jnp.where(mine, inten_grad[k], 0.0)], axis=0
         )
@@ -318,78 +367,65 @@
     gd_slot[...] = slot_grad[:n] * (1.0 / (1.0 + jnp.exp(-e0)))
     gi_slot[...] = slot_grad[n:] * (inten_all * (1.0 - inten_all))
 
-    w1_acc[...] = jnp.zeros_like(w1_acc)
-    small_acc[...] = jnp.zeros_like(small_acc)
-
-    def head_back(w, out_ref, at):
-        g0 = gd_slot[pl.ds(w, 1), :]
-        g1 = gi_slot[pl.ds(w, 1), :]
-        value = hid_val[w]
-        grad = (w2[:, 0:1] * g0 + w2[:, 1:2] * g1) * hid_slope[w]
+    w1_acc = jnp.zeros((ch, 3 * hid), F32)
+    small = [jnp.zeros((hid, 1), F32)] * 3
+    for k in [*range(1, n), 0]:
+        g0 = gd_slot[k : k + 1, :]
+        g1 = gi_slot[k : k + 1, :]
+        value = hid_val[k]
+        grad = (w2_density * g0 + w2_intensity * g1) * hid_slope[k]
         pieces = jnp.concatenate([p.astype(BF16) for p in split(grad, 3)], axis=0)
-        out_ref[at] = matmul(w1_rep[...], pieces)
-        w1_acc[...] += matmul_nt(rep_recv[w], pieces)
-        small_acc[0] += jnp.sum(grad, axis=1, keepdims=True)
-        small_acc[1] += jnp.sum(value * g0, axis=1, keepdims=True)
-        small_acc[2] += jnp.sum(value * g1, axis=1, keepdims=True)
-
-    @pl.loop(1, n)
-    def _(k):
-        w = lax.rem(sector + k, n)
-        head_back(w, grad_send, w)
-        to_sector(grad_send, grad_recv, grad_sems, k).start()
-
-    head_back(sector, grad_recv, sector)
-
-    cell_grad[...] = jnp.zeros_like(cell_grad)
-
-    def scatter_from(v):
-        brick = jnp.broadcast_to(addr[v] >> (cells.bit_length() - 1), (ch, cap))
-        high, low = split(grad_recv[v], 2)
+        if k > 0:
+            grad_send[k] = matmul(w1_rep[...], pieces)
+            give_back(k).start()
+        else:
+            grad_recv[k] = matmul(w1_rep[...], pieces)
+        w1_acc = w1_acc + matmul_nt(rep_recv[k], pieces)
+        terms = (grad, value * g0, value * g1)
+        small = [a + jnp.sum(t, axis=1, keepdims=True) for a, t in zip(small, terms)]
+
+    for k in range(n):
+        if k > 0:
+            give_back(k).wait()
+        brick = jnp.broadcast_to(addr[k] >> (cells.bit_length() - 1), (ch, cap))
+        high, low = split(grad_recv[k], 2)
         spread = jnp.concatenate(
             [jnp.where(brick == b, p, 0.0).astype(BF16) for p in (high, low) for b in range(nb)],
             axis=0,
         )
-        added = matmul_nt(spread, addr_hot[v])
-        cell_grad[...] += added[: nb * ch] + added[nb * ch :]
-
-    scatter_from(sector)
-
-    @pl.loop(1, n)
-    def _(k):
-        to_sector(grad_send, grad_recv, grad_sems, k).wait()
-        scatter_from(lax.rem(sector + n - k, n))
-
-    wgrad[...] = jnp.zeros_like(wgrad)
-    wide = wgrad.shape[1]
+        added = matmul_nt(spread, addr_hot[k])
+        added = added[: nb * ch] + added[nb * ch :]
+        cell_grad[...] = added if k == 0 else cell_grad[...] + added
+
     used = 27 * ch
-
-    def conv_back(b, bias):
-        def put(k, value):
-            cols[pl.ds(k * ch, ch), :] = value
-
-        at = pl.ds(pl.multiple_of(b * ch, ch), ch)
+    wide = -(-used // 128) * 128
+    wgrad = jnp.zeros((ch, used), F32)
+    bias_grad = jnp.zeros((ch, 1), F32)
+    for b in range(nb):
+
+        def put(k, value, b=b):
+            cot_cols[b, k * ch : (k + 1) * ch, :] = value
+
+        at = slice(b * ch, (b + 1) * ch)
         cot = (cell_grad[at, :] * slope_conv[at, :]).astype(BF16)
         unfold(cot.astype(F32), put)
-        grad_bricks[b] = matmul(conv_back_w[...], cols[...]).astype(BF16)
-        wgrad[:, :used] += matmul_nt(bricks[b], cols[...])
-        return bias + jnp.sum(cot.astype(F32), axis=1, keepdims=True)
-
-    bias_grad = lax.fori_loop(0, nb, conv_back, jnp.zeros((ch, 1), F32))
+        grad_bricks[b] = matmul(conv_back_w[...], cot_cols[b]).astype(BF16)
+        wgrad = wgrad + matmul_nt(cot, cols[b])
+        bias_grad = bias_grad + jnp.sum(cot.astype(F32), axis=1, keepdims=True)
 
     tiles = wide // 128
+    wgrad = jnp.concatenate([wgrad, jnp.zeros((ch, wide - used), F32)], axis=1)
     for t in range(tiles):
         for part in range(ch // 8):
             pack[t * (ch // 8) + part] = wgrad[part * 8 : part * 8 + 8, t * 128 : t * 128 + 128]
     lane = lax.broadcasted_iota(jnp.int32, (ch, 128), 1)
-    w1_all = w1_acc[...]
-    w1_grad = w1_all[:, :hid] + w1_all[:, hid : 2 * hid] + w1_all[:, 2 * hid :]
+    w1_grad = w1_acc[:, :hid] + w1_acc[:, hid : 2 * hid] + w1_acc[:, 2 * hid :]
     last = jnp.concatenate([w1_grad, jnp.zeros((ch, 128 - hid), F32)], axis=1)
     place = hid
     for j in range(3):
         for part in range(hid // ch):
-            column = small_acc[j, part * ch : (part + 1) * ch, :]
-            last = last + jnp.where(lane == place, column, 0.0)
+            values = small[j][part * ch : (part + 1) * ch, :]
+            last = last + jnp.where(lane == place, values, 0.0)
             place += 1
     last = last + jnp.where(lane == place, bias_grad, 0.0)
     loss_here = jnp.where(shell == 0, loss, 0.0)
@@ -441,6 +477,53 @@
     @pl.loop(1, count)
     def _(k):
         to_everyone(k).wait()
+
+
+def finish(
+    scale,
+    reduced,
+    grad_bricks,
+    ray_depth,
+    loss_out,
+    conv_out,
+    conv_b_out,
+    w1_out,
+    b1_out,
+    w2_out,
+    bricks_out,
+    depth_out,
+):
+    ch, used = conv_out.shape
+    hid = w1_out.shape[1]
+    per = ch // 8
+    tiles = -(-used // 128)
+    for t in range(tiles):
+        stop = min(128, used - t * 128)
+        for part in range(per):
+            conv_out[part * 8 : part * 8 + 8, t * 128 : t * 128 + stop] = reduced[
+                t * per + part, :, :stop
+            ]
+    last = jnp.concatenate([reduced[tiles * per + part] for part in range(per)], axis=0)
+    w1_out[...] = last[:, :hid]
+
+    def row(place, count):
+        i = lax.broadcasted_iota(jnp.int32, (ch, ch * count), 0)
+        j = lax.broadcasted_iota(jnp.int32, (ch, ch * count), 1)
+        total = jnp.zeros((1, ch * count), F32)
+        for part in range(count):
+            spread = jnp.where(j == i + part * ch, last[:, place + part : place + part + 1], 0.0)
+            total = total + jnp.sum(spread, axis=0, keepdims=True)
+        return total
+
+    count = hid // ch
+    b1_out[...] = row(hid, count)
+    w2_out[0:1, :] = row(hid + count, count)
+    w2_out[1:2, :] = row(hid + 2 * count, count)
+    place = hid + 3 * count
+    conv_b_out[...] = row(place, 1)
+    loss_out[...] = last[0:1, place + 1 : place + 2] * scale
+    bricks_out[...] = grad_bricks[...]
+    depth_out[...] = ray_depth[...]
 
 
 def local(
@@ -463,22 +546,17 @@
     cap = queries.shape[2]
     hid = head_w1.shape[1]
     rays = depth_target.shape[0]
-    wide = -(-27 * ch // 128) * 128
-    chunks = (wide // 128 + 1) * (ch // 8)
-    held = max(count, -(-chunks // count) * count)
-    assert held == count and cap & (cap - 1) == 0 and cells == 512
-    conv_back_w = conv_w.reshape(ch, 27, ch)[:, ::-1].transpose(2, 1, 0).reshape(ch, 27 * ch)
+    chunks = (-(-27 * ch // 128) + 1) * (ch // 8)
+    assert chunks <= count and cap & (cap - 1) == 0 and cells == 512 and rays % 128 == 0
     operands = (
         bricks[0],
         conv_w,
-        conv_back_w,
-        conv_b[:, None],
-        head_w1.T,
-        jnp.concatenate([head_w1] * 3, axis=1),
-        head_b1[:, None],
-        head_w2,
-        queries[0][:, None, :],
-        sample_src[0].reshape(rays, SAMP).T[:, None, :],
+        conv_b[None],
+        head_w1,
+        head_b1[None],
+        head_w2.T,
+        queries[0],
+        sample_src,
         depth_target[None],
         inten_target[None],
         drop_label[None],
@@ -490,15 +568,21 @@
         out_shape=(
             jax.ShapeDtypeStruct((nb, ch, cells), BF16),
             jax.ShapeDtypeStruct((1, rays), F32),
-            jax.ShapeDtypeStruct((held, 8, 128), F32),
+            jax.ShapeDtypeStruct((count, 8, 128), F32),
         ),
         in_specs=[vmem] * len(operands),
         out_specs=(vmem, vmem, vmem),
         scratch_shapes=[
+            pltpu.VMEM((ch, 27 * ch), BF16),
+            pltpu.VMEM((hid, ch), BF16),
+            pltpu.VMEM((ch, 3 * hid), BF16),
+            pltpu.VMEM((SAMP, rays), jnp.int32),
+            pltpu.VMEM((n, 1, cap), jnp.int32),
             pltpu.VMEM((n, 1, cap), jnp.int32),
             pltpu.VMEM((nb * ch, cells), BF16),
             pltpu.VMEM((nb * ch, cells), F32),
-            pltpu.VMEM((27 * ch, cells), BF16),
+            pltpu.VMEM((nb, 27 * ch, cells), BF16),
+            pltpu.VMEM((nb, 27 * ch, cells), BF16),
             pltpu.VMEM((n, cells, cap), BF16),
             pltpu.VMEM((SAMP, cap, rays), BF16),
             pltpu.VMEM((n, ch, cap), BF16),
@@ -513,11 +597,8 @@
             pltpu.VMEM((n, ch, cap), F32),
             pltpu.VMEM((n, ch, cap), F32),
             pltpu.VMEM((nb * ch, cells), F32),
-            pltpu.VMEM((held, 8, 128), F32),
             pltpu.VMEM((count, 8, 128), F32),
-            pltpu.VMEM((ch, wide), F32),
-            pltpu.VMEM((ch, 3 * hid), F32),
-            pltpu.VMEM((3, hid, 1), F32),
+            pltpu.VMEM((count, 8, 128), F32),
             dma((2, n)),
             dma((2, n)),
             dma((2, shells)),
@@ -530,21 +611,28 @@
             collective_id=0, has_side_effects=True, vmem_limit_bytes=56 * 1024 * 1024
         ),
     )(*operands)
-    tiles = wide // 128
-    flat = reduced.reshape(-1, 128)
-    conv_grad = flat[: tiles * ch].reshape(tiles, ch, 128).transpose(1, 0, 2).reshape(ch, wide)
-    conv_grad = conv_grad[:, : 27 * ch].reshape(ch, 27, ch)[:, ::-1].transpose(2, 1, 0)
-    last = flat[tiles * ch : (tiles + 1) * ch]
-    per = hid // ch
-    columns = last[:, hid : hid + 3 * per].T.reshape(3, hid)
-    place = hid + 3 * per
+    loss, conv_grad, conv_b_grad, w1_grad, b1_grad, w2_grad, grad_bricks, ray_depth = pl.pallas_call(
+        functools.partial(finish, 1.0 / (rays * n)),
+        out_shape=(
+            jax.ShapeDtypeStruct((1, 1), F32),
+            jax.ShapeDtypeStruct((ch, 27 * ch), F32),
+            jax.ShapeDtypeStruct((1, ch), F32),
+            jax.ShapeDtypeStruct((ch, hid), F32),
+            jax.ShapeDtypeStruct((1, hid), F32),
+            jax.ShapeDtypeStruct((2, hid), F32),
+            jax.ShapeDtypeStruct((nb, ch, cells), BF16),
+            jax.ShapeDtypeStruct((1, rays), F32),
+        ),
+        in_specs=[vmem] * 3,
+        out_specs=(vmem,) * 8,
+    )(reduced, grad_bricks, ray_depth)
     return (
-        last[0, place + 1] / (rays * n),
-        conv_grad.reshape(ch, 27 * ch),
-        last[:, place],
-        last[:, :hid],
-        columns[0],
-        columns[1:].T,
+        loss[0, 0],
+        conv_grad,
+        conv_b_grad[0],
+        w1_grad,
+        b1_grad[0],
+        w2_grad.T,
         grad_bricks[None],
         ray_depth[0],
     )

time: 85.4 us -> 66.7 us (0.78)
  local copies, waits for them, and re-layouts: 16.4 us -> 0 us
  between operations: 2.52 us -> 0.65 us
  other arithmetic: 1.37 us -> 0 us
  Pallas kernels: 64.8 us -> 65.9 us
    unnamed x24 -> x0, local copies, waits for them, and re-layouts: 4.54 us -> none
    slice x8 -> x0, local copies, waits for them, and re-layouts: 3.78 us -> none  [the longest x1 0.91 us: local(): flat[:tiles * ch].reshape(tiles, ch, 128).transpose(1, 0, 2)]
    reshape x5 -> x0, local copies, waits for them, and re-layouts: 2.98 us -> none  [the longest x2 1.9 us: local(): conv_w.reshape(ch, 27, ch)[:, ::-1].transpose(2, 1, 0).reshape(ch, 27 * ch)]
    broadcast_in_dim x3 -> x0, local copies, waits for them, and re-layouts: 2.02 us -> none  [the longest x1 0.71 us: local(): head_b1[:, None]]
    pallas_call x0 -> x1, Pallas kernels: none -> 1.82 us  [local(): pl.pallas_call(functools.partial(finish, 1.0 / (rays * n)), out_shape=(ja...]
    transpose x3 -> x0, local copies, waits for them, and re-layouts: 1.19 us -> none  [the longest x1 0.56 us: local(): conv_grad[:, :27 * ch].reshape(ch, 27, ch)[:, ::-1].transpose(2, 1, 0)]
    another operation x3 -> x0, local copies, waits for them, and re-layouts: 0.88 us -> none  [the longest x1 0.63 us: local(): queries[0][:, None, :]]
where the time goes in v1:
time: 66.7 us; the launch traced here: 66.5 us
  Pallas kernels  65.9 us (99%)
    pallas_call x1, Pallas kernels, local(): pl.pallas_call(functools.partial(body, shells, n), out_shape=(jax.ShapeDt...  64.1 us
    pallas_call x1, Pallas kernels, local(): pl.pallas_call(functools.partial(finish, 1.0 / (rays * n)), out_shape=(ja...  1.82 us

profile of v1, /device:TPU:0, one launch (start us, length us, event | category | flops | bytes accessed | tf_op | source)
XLA Modules:
  0.0 66.5 jit_solution(10579714202888919060)
XLA Ops:
  0.6 64.1 %shard_map.170 = (bf16[8,32,512]{2,1,0:T(8,128)(2,1)}, f32[1,512]{1,0:T(1,128)}, f32[32,8,128]{2,1,0:T(8,128)}) custom-call(bf16[8,32,512]{2,1,0:T(8,128)(2,1)} %bitcast.14, bf16[32,864]{1,0:T(8,128)(2,1)} %conv_w.1, f32[1,32]{1,0:T(1,128)} %bitcast.20, bf16[32,64]{1,0:T(8,128)(2,1)} %w1.1, f32[1,64]{1,0:T(1,128)} %bitcast.21, f32[2,64]{1,0:T(2,128)} %bitcast.19, ...), custom_call_target="tpu_custom_call" | custom-call | tf_op jit(solution)/shard_map/pallas_call | solution.py:566
  64.7 1.8 %shard_map.171 = (f32[1,1]{1,0:T(1,128)}, f32[32,864]{1,0:T(8,128)}, f32[1,32]{1,0:T(1,128)}, f32[32,64]{1,0:T(8,128)}, f32[1,64]{1,0:T(1,128)}, /*index=5*/f32[...) custom-call(f32[32,8,128]{2,1,0:T(8,128)} %get-tuple-element.19.reduced, ...), custom_call_target="tpu_custom_call" | custom-call | tf_op jit(solution)/shard_map/pallas_call | solution.py:614

commit v2 on v1

--- a/solution.py
+++ b/solution.py
@@ -42,28 +42,22 @@
     return lax.dot_general(a, b, NT, preferred_element_type=F32)
 
 
-def shifted(x, step, coord):
-    width = x.shape[1]
-    out = []
-    for move in (-1, 0, 1):
-        if move == 0:
-            out.append(x)
-        else:
-            rolled = pltpu.roll(x, (-move * step) % width, 1)
-            inside = coord >= 1 if move < 0 else coord <= 6
-            out.append(rolled * jnp.where(inside, 1.0, 0.0))
-    return out
-
-
-def unfold(x, put):
-    lane = lax.broadcasted_iota(jnp.int32, (1, x.shape[1]), 1)
-    by_c = shifted(x, 1, lane & 7)
+def moved(x, step, coord, move):
+    if move == 0:
+        return x
+    rolled = pltpu.roll(x, (-move * step) % x.shape[1], 1)
+    inside = coord >= 1 if move < 0 else coord <= 6
+    return rolled * jnp.where(inside, 1.0, 0.0)
+
+
+def unfold(x, out, lane):
+    ch = x.shape[0]
     for c in range(3):
-        by_b = shifted(by_c[c], 8, (lane >> 3) & 7)
+        by_c = moved(x, 1, lane & 7, c - 1)
         for b in range(3):
-            by_a = shifted(by_b[b], 64, lane >> 6)
-            for a in range(3):
-                put(9 * a + 3 * b + c, by_a[a].astype(BF16))
+            k = 3 * b + c
+            value = moved(by_c, 8, (lane >> 3) & 7, b - 1)
+            out[k * ch : (k + 1) * ch, :] = value.astype(BF16)
 
 
 def column(row):
@@ -97,39 +91,27 @@
     grad_bricks,
     ray_depth_out,
     reduced,
-    conv_back_w,
-    w1_t,
-    w1_rep,
     sources,
-    asked,
-    addr,
     decoded,
     slope_conv,
     cols,
     cot_cols,
-    addr_hot,
-    src_hot,
-    rep_send,
-    rep_recv,
-    hid_val,
-    hid_slope,
-    dens_slot,
-    inten_slot,
-    gd_slot,
-    gi_slot,
+    cots,
+    hot,
+    hid_x,
+    hid_t,
+    own_table,
+    tables,
     shell_buf,
-    grad_send,
-    grad_recv,
-    cell_grad,
+    cell_send,
+    cell_recv,
     pack,
     red_recv,
-    req_sems,
-    rep_sems,
+    table_sems,
     shell_sems,
-    grad_sems,
+    cell_sems,
     red_sems,
     out_sems,
-    own_sem,
 ):
     n = sectors
     count = shells * sectors
@@ -137,10 +119,13 @@
     cap = queries.shape[1]
     hid = w1.shape[1]
     rays = sources.shape[1]
-    shift = cap.bit_length() - 1
+    groups = nb * cells // 256
+    halves = cells // 256
     shell = lax.axis_index("shell")
     sector = lax.axis_index("sector")
     me = shell * n + sector
+    lane = lax.broadcasted_iota(jnp.int32, (1, cells), 1)
+    plane = lane >> 6
 
     def flat_peer(k):
         peer = lax.rem(me + k, count)
@@ -153,17 +138,26 @@
         _, where = flat_peer(k)
         pl.semaphore_signal(barrier, inc=1, device_id=where, device_id_type=MESH)
 
-    for j in range(n):
-        asked[j] = queries[j : j + 1, :]
     conv_b_col = column(conv_b[...])
     b1_col = column(b1[...])
     w2_density = column(w2[0:1, :])
     w2_intensity = column(w2[1:2, :])
-    w1_t[...] = matmul_nt(repeated_eye(hid, 1), w1[...]).astype(BF16)
-    w1_rep[...] = matmul(w1[...], repeated_eye(hid, 3)).astype(BF16)
-    turned = jnp.transpose(conv_w[...].astype(F32))
-    conv_back_w[...] = jnp.concatenate(
-        [turned[k * ch : (k + 1) * ch] for k in reversed(range(27))], axis=1
+    w1_t = matmul_nt(repeated_eye(hid, 1), w1[...]).astype(BF16)
+    w1_rep = matmul(w1[...], repeated_eye(hid, 3)).astype(BF16)
+    wide_w = conv_w[...].astype(F32)
+    width = 9 * ch
+    conv_rows = jnp.concatenate(
+        [wide_w[:, a * width : (a + 1) * width] for a in range(3)], axis=0
+    ).astype(BF16)
+    turned = jnp.transpose(wide_w)
+    back_rows = jnp.concatenate(
+        [
+            jnp.concatenate(
+                [turned[(9 * a + 8 - k) * ch : (9 * a + 9 - k) * ch] for k in range(9)], axis=1
+            )
+            for a in range(3)
+        ],
+        axis=0,
     ).astype(BF16)
     block = SAMP * 128
     ray_of = lax.broadcasted_iota(jnp.int32, (block, 128), 0) // SAMP
@@ -179,105 +173,89 @@
         whole = got[:SAMP] * 128.0 + got[SAMP:]
         sources[:, j * 128 : (j + 1) * 128] = whole.astype(jnp.int32)
 
+    sig_density = []
+    intensity_here = []
+    for b in range(nb):
+        unfold(bricks[b].astype(F32), cols.at[b], lane)
+        by_a = matmul(conv_rows, cols[b])
+        pre = conv_b_col
+        for a in range(3):
+            pre = pre + moved(by_a[a * ch : (a + 1) * ch], 64, plane, a - 1)
+        value, slope = gelu_and_slope(pre)
+        feats = value.astype(BF16)
+        decoded[b] = feats
+        slope_conv[b] = slope
+        x = matmul(w1_t, feats) + b1_col
+        t = jnp.tanh(GELU_SCALE * (x + GELU_CUBIC * (x * (x * x))))
+        hid_x[b] = x
+        hid_t[b] = t
+        value = x * (0.5 * (1.0 + t))
+        e0 = jnp.sum(value * w2_density, axis=0, keepdims=True)
+        e1 = jnp.sum(value * w2_intensity, axis=0, keepdims=True)
+        density = jnp.maximum(e0, 0.0) + jnp.log1p(jnp.exp(-jnp.abs(e0)))
+        sig_density.append(1.0 / (1.0 + jnp.exp(-e0)))
+        intensity_here.append(1.0 / (1.0 + jnp.exp(-e1)))
+        for h in range(halves):
+            row = b * halves + h
+            at = slice(h * 256, (h + 1) * 256)
+            own_table[row : row + 1, :] = density[:, at]
+            own_table[groups + row : groups + row + 1, :] = intensity_here[b][:, at]
+
     pl.semaphore_wait(barrier, count - 1)
 
-    def to_owner(src, dst, sems, k):
+    def give_table(k):
         return pltpu.make_async_remote_copy(
-            src_ref=src,
-            dst_ref=dst.at[k],
-            send_sem=sems.at[0, k],
-            recv_sem=sems.at[1, k],
+            src_ref=own_table,
+            dst_ref=tables.at[sector],
+            send_sem=table_sems.at[0, k],
+            recv_sem=table_sems.at[1, k],
             device_id={"shell": shell, "sector": lax.rem(sector + k, n)},
             device_id_type=MESH,
         )
 
-    def to_asker(src, dst, sems, k):
-        return pltpu.make_async_remote_copy(
-            src_ref=src,
-            dst_ref=dst.at[k],
-            send_sem=sems.at[0, k],
-            recv_sem=sems.at[1, k],
-            device_id={"shell": shell, "sector": lax.rem(sector + n - k, n)},
-            device_id_type=MESH,
-        )
-
-    def request(k):
-        return to_owner(asked.at[lax.rem(sector + k, n)], addr, req_sems, k)
-
-    def reply(k):
-        return to_asker(rep_send.at[k], rep_recv, rep_sems, k)
-
-    def give_back(k):
-        return to_owner(grad_send.at[k], grad_recv, grad_sems, k)
-
     for k in range(1, n):
-        request(k).start()
-
-    own = pltpu.make_async_copy(asked.at[sector], addr.at[0], own_sem)
-    own.start()
-
-    for b in range(nb):
-
-        def put(k, value, b=b):
-            cols[b, k * ch : (k + 1) * ch, :] = value
-
-        unfold(bricks[b].astype(F32), put)
-        value, slope = gelu_and_slope(matmul(conv_w[...], cols[b]) + conv_b_col)
-        decoded[b * ch : (b + 1) * ch, :] = value.astype(BF16)
-        slope_conv[b * ch : (b + 1) * ch, :] = slope
-
-    own.wait()
+        give_table(k).start()
+    tables[sector] = own_table[...]
+
+    asked = queries[...]
+    parts = cap // 256
+    asked = jnp.concatenate([asked[:, h * 256 : (h + 1) * 256] for h in range(parts)], axis=0)
+    asked = jnp.concatenate([(asked >> 6).astype(F32), (asked & 63).astype(F32)], axis=0)
+    asked = asked.astype(BF16)
+    held = parts * n
+    place_of = lax.broadcasted_iota(jnp.int32, (256, rays), 0)
+    held_of = lax.broadcasted_iota(jnp.int32, (held, rays), 0)
+    codes = []
+    for k in range(SAMP):
+        src = sources[k : k + 1, :]
+        owner = src >> (cap.bit_length() - 1)
+        got = matmul(asked, jnp.where(place_of == (src & 255), 1.0, 0.0).astype(BF16))
+        got = got[:held] * 64.0 + got[held:]
+        mine = held_of == ((src >> 8) & (parts - 1)) * n + owner
+        address = jnp.sum(jnp.where(mine, got, 0.0), axis=0, keepdims=True).astype(jnp.int32)
+        hot[k] = jnp.where(place_of == (address & 255), 1.0, 0.0).astype(BF16)
+        codes.append(owner * groups + (address >> 8))
+
     for k in range(1, n):
-        request(k).wait()
-
-    def gather_for(k, out_ref):
-        where = addr[k]
-        cell = where & (cells - 1)
-        brick = jnp.broadcast_to(where >> (cells.bit_length() - 1), (ch, cap))
-        rows = lax.broadcasted_iota(jnp.int32, (cells, cap), 0)
-        addr_hot[k] = jnp.where(rows == cell, 1.0, 0.0).astype(BF16)
-        picked = matmul(decoded[...], addr_hot[k])
-        feats = jnp.zeros((ch, cap), F32)
-        for b in range(nb):
-            feats = feats + jnp.where(brick == b, picked[b * ch : (b + 1) * ch], 0.0)
-        out_ref[k] = feats.astype(BF16)
-
-    for k in range(1, n):
-        gather_for(k, rep_send)
-        reply(k).start()
-    gather_for(0, rep_recv)
-
-    for k in range(SAMP):
-        rows = lax.broadcasted_iota(jnp.int32, (cap, rays), 0)
-        slot = sources[k : k + 1, :] & (cap - 1)
-        src_hot[k] = jnp.where(rows == slot, 1.0, 0.0).astype(BF16)
-
-    for k in range(n):
-        if k > 0:
-            reply(k).wait()
-        value, slope = gelu_and_slope(matmul(w1_t[...], rep_recv[k]) + b1_col)
-        hid_val[k] = value
-        hid_slope[k] = slope
-        dens_slot[k : k + 1, :] = jnp.sum(value * w2_density, axis=0, keepdims=True)
-        inten_slot[k : k + 1, :] = jnp.sum(value * w2_intensity, axis=0, keepdims=True)
-
-    e0 = dens_slot[...]
-    e1 = inten_slot[...]
-    dens_all = jnp.maximum(e0, 0.0) + jnp.log1p(jnp.exp(-jnp.abs(e0)))
-    inten_all = 1.0 / (1.0 + jnp.exp(-e1))
-    slots = jnp.concatenate([dens_all, inten_all], axis=0)
-    slot_pieces = jnp.concatenate([p.astype(BF16) for p in split(slots, 3)], axis=0)
-    owner_rows = lax.broadcasted_iota(jnp.int32, (n, rays), 0)
-    owner_of = (sources[...] >> shift) - sector
-    owner_of = jnp.where(owner_of < 0, owner_of + n, owner_of)
+        give_table(k).wait()
+
+    everything = tables[...].reshape(n * 2 * groups, 256)
+    everything = jnp.concatenate([p.astype(BF16) for p in split(everything, 2)], axis=0)
+    group_of = lax.broadcasted_iota(jnp.int32, (groups, rays), 0)
+    total = n * 2 * groups
     dens = []
     inten = []
     for k in range(SAMP):
-        got = matmul(slot_pieces, src_hot[k])
-        got = got[: 2 * n] + got[2 * n : 4 * n] + got[4 * n :]
-        mine = owner_rows == owner_of[k : k + 1, :]
-        dens.append(jnp.sum(jnp.where(mine, got[:n], 0.0), axis=0, keepdims=True))
-        inten.append(jnp.sum(jnp.where(mine, got[n:], 0.0), axis=0, keepdims=True))
+        got = matmul(everything, hot[k])
+        got = got[:total] + got[total:]
+        sums = [jnp.zeros((groups, rays), F32)] * 2
+        for w in range(n):
+            mine = group_of == codes[k] - w * groups
+            for j in range(2):
+                at = (2 * w + j) * groups
+                sums[j] = sums[j] + jnp.where(mine, got[at : at + groups], 0.0)
+        dens.append(jnp.sum(sums[0], axis=0, keepdims=True))
+        inten.append(jnp.sum(sums[1], axis=0, keepdims=True))
 
     step_size = 2.0 / (shells * SAMP)
     span = 1.0 / (shells * SAMP)
@@ -312,6 +290,15 @@
 
     for k in range(1, shells):
         to_shell(k).start()
+    for b in range(nb):
+        x = hid_x[b]
+        t = hid_t[b]
+        half = 0.5 * (1.0 + t)
+        hid_x[b] = x * half
+        hid_t[b] = half + 0.5 * x * (1.0 - t * t) * (
+            GELU_SCALE * (1.0 + 3.0 * GELU_CUBIC * (x * x))
+        )
+
     for k in range(1, shells):
         to_shell(k).wait()
 
@@ -355,81 +342,93 @@
         inten_grad[k] = cot_light * weight[k]
         dens_grad[k] = step_size * (pull * enter[k] * leave[k] - later + cot_tau)
         later = later + pull * weight[k]
-    slot_grad = jnp.zeros((6 * n, cap), F32)
+
+    table_grad = jnp.zeros((2 * total, 256), F32)
     for k in range(SAMP):
-        mine = owner_rows == owner_of[k : k + 1, :]
-        both = jnp.concatenate(
-            [jnp.where(mine, dens_grad[k], 0.0), jnp.where(mine, inten_grad[k], 0.0)], axis=0
+        masks = [group_of == codes[k] - w * groups for w in range(n)]
+        pair = [split(dens_grad[k], 2), split(inten_grad[k], 2)]
+        spread = jnp.concatenate(
+            [
+                jnp.where(masks[w], pair[j][p], 0.0).astype(BF16)
+                for p in range(2)
+                for w in range(n)
+                for j in range(2)
+            ],
+            axis=0,
         )
-        both = jnp.concatenate([p.astype(BF16) for p in split(both, 3)], axis=0)
-        slot_grad = slot_grad + matmul_nt(both, src_hot[k])
-    slot_grad = slot_grad[: 2 * n] + slot_grad[2 * n : 4 * n] + slot_grad[4 * n :]
-    gd_slot[...] = slot_grad[:n] * (1.0 / (1.0 + jnp.exp(-e0)))
-    gi_slot[...] = slot_grad[n:] * (inten_all * (1.0 - inten_all))
+        table_grad = table_grad + matmul_nt(spread, hot[k])
+    table_grad = table_grad[:total] + table_grad[total:]
+    cell_send[...] = table_grad.reshape(n, 2 * groups, 256)
+
+    def give_back(k):
+        peer = lax.rem(sector + k, n)
+        return pltpu.make_async_remote_copy(
+            src_ref=cell_send.at[peer],
+            dst_ref=cell_recv.at[sector],
+            send_sem=cell_sems.at[0, k],
+            recv_sem=cell_sems.at[1, k],
+            device_id={"shell": shell, "sector": peer},
+            device_id_type=MESH,
+        )
+
+    for k in range(1, n):
+        give_back(k).start()
+    cell_recv[sector] = cell_send[sector]
+    for k in range(1, n):
+        give_back(k).wait()
+    table_grad = jnp.sum(cell_recv[...], axis=0)
 
     w1_acc = jnp.zeros((ch, 3 * hid), F32)
     small = [jnp.zeros((hid, 1), F32)] * 3
-    for k in [*range(1, n), 0]:
-        g0 = gd_slot[k : k + 1, :]
-        g1 = gi_slot[k : k + 1, :]
-        value = hid_val[k]
-        grad = (w2_density * g0 + w2_intensity * g1) * hid_slope[k]
+    wgrad = jnp.zeros((3 * ch, width), F32)
+    bias_grad = jnp.zeros((ch, 1), F32)
+    for b in range(nb):
+        rows = [
+            jnp.concatenate(
+                [
+                    table_grad[j * groups + b * halves + h : j * groups + b * halves + h + 1]
+                    for h in range(halves)
+                ],
+                axis=1,
+            )
+            for j in range(2)
+        ]
+        g0 = rows[0] * sig_density[b]
+        g1 = rows[1] * (intensity_here[b] * (1.0 - intensity_here[b]))
+        value = hid_x[b]
+        grad = (w2_density * g0 + w2_intensity * g1) * hid_t[b]
         pieces = jnp.concatenate([p.astype(BF16) for p in split(grad, 3)], axis=0)
-        if k > 0:
-            grad_send[k] = matmul(w1_rep[...], pieces)
-            give_back(k).start()
-        else:
-            grad_recv[k] = matmul(w1_rep[...], pieces)
-        w1_acc = w1_acc + matmul_nt(rep_recv[k], pieces)
+        w1_acc = w1_acc + matmul_nt(decoded[b], pieces)
         terms = (grad, value * g0, value * g1)
         small = [a + jnp.sum(t, axis=1, keepdims=True) for a, t in zip(small, terms)]
-
-    for k in range(n):
-        if k > 0:
-            give_back(k).wait()
-        brick = jnp.broadcast_to(addr[k] >> (cells.bit_length() - 1), (ch, cap))
-        high, low = split(grad_recv[k], 2)
-        spread = jnp.concatenate(
-            [jnp.where(brick == b, p, 0.0).astype(BF16) for p in (high, low) for b in range(nb)],
-            axis=0,
-        )
-        added = matmul_nt(spread, addr_hot[k])
-        added = added[: nb * ch] + added[nb * ch :]
-        cell_grad[...] = added if k == 0 else cell_grad[...] + added
-
-    used = 27 * ch
-    wide = -(-used // 128) * 128
-    wgrad = jnp.zeros((ch, used), F32)
-    bias_grad = jnp.zeros((ch, 1), F32)
-    for b in range(nb):
-
-        def put(k, value, b=b):
-            cot_cols[b, k * ch : (k + 1) * ch, :] = value
-
-        at = slice(b * ch, (b + 1) * ch)
-        cot = (cell_grad[at, :] * slope_conv[at, :]).astype(BF16)
-        unfold(cot.astype(F32), put)
-        grad_bricks[b] = matmul(conv_back_w[...], cot_cols[b]).astype(BF16)
-        wgrad = wgrad + matmul_nt(cot, cols[b])
-        bias_grad = bias_grad + jnp.sum(cot.astype(F32), axis=1, keepdims=True)
-
-    tiles = wide // 128
-    wgrad = jnp.concatenate([wgrad, jnp.zeros((ch, wide - used), F32)], axis=1)
+        cot = (matmul(w1_rep, pieces) * slope_conv[b]).astype(BF16)
+        exact = cot.astype(F32)
+        cots[b] = cot
+        by_a = [moved(exact, 64, plane, 1 - a).astype(BF16) for a in range(3)]
+        wgrad = wgrad + matmul_nt(jnp.concatenate(by_a, axis=0), cols[b])
+        bias_grad = bias_grad + jnp.sum(exact, axis=1, keepdims=True)
+
+    tiles = -(-27 * ch // 128)
+    wgrad = jnp.concatenate(
+        [wgrad[a * ch : (a + 1) * ch] for a in range(3)]
+        + [jnp.zeros((ch, tiles * 128 - 27 * ch), F32)],
+        axis=1,
+    )
     for t in range(tiles):
         for part in range(ch // 8):
             pack[t * (ch // 8) + part] = wgrad[part * 8 : part * 8 + 8, t * 128 : t * 128 + 128]
-    lane = lax.broadcasted_iota(jnp.int32, (ch, 128), 1)
+    at_lane = lax.broadcasted_iota(jnp.int32, (ch, 128), 1)
     w1_grad = w1_acc[:, :hid] + w1_acc[:, hid : 2 * hid] + w1_acc[:, 2 * hid :]
     last = jnp.concatenate([w1_grad, jnp.zeros((ch, 128 - hid), F32)], axis=1)
     place = hid
     for j in range(3):
         for part in range(hid // ch):
             values = small[j][part * ch : (part + 1) * ch, :]
-            last = last + jnp.where(lane == place, values, 0.0)
+            last = last + jnp.where(at_lane == place, values, 0.0)
             place += 1
-    last = last + jnp.where(lane == place, bias_grad, 0.0)
+    last = last + jnp.where(at_lane == place, bias_grad, 0.0)
     loss_here = jnp.where(shell == 0, loss, 0.0)
-    last = last + jnp.where(lane == place + 1, loss_here, 0.0)
+    last = last + jnp.where(at_lane == place + 1, loss_here, 0.0)
     base = tiles * (ch // 8)
     for part in range(ch // 8):
         pack[base + part] = last[part * 8 : part * 8 + 8]
@@ -464,6 +463,17 @@
 
     red_recv[me] = pack[me]
 
+    def brick_back(b):
+        unfold(cots[b].astype(F32), cot_cols.at[b], lane)
+        by_a = matmul(back_rows, cot_cols[b])
+        grad = jnp.zeros((ch, cells), F32)
+        for a in range(3):
+            grad = grad + moved(by_a[a * ch : (a + 1) * ch], 64, plane, 1 - a)
+        grad_bricks[b] = grad.astype(BF16)
+
+    for b in range(nb // 2):
+        brick_back(b)
+
     @pl.loop(1, count)
     def _(k):
         to_reducer(k).wait()
@@ -473,6 +483,9 @@
     @pl.loop(1, count)
     def _(k):
         to_everyone(k).start()
+
+    for b in range(nb // 2, nb):
+        brick_back(b)
 
     @pl.loop(1, count)
     def _(k):
@@ -546,8 +559,9 @@
     cap = queries.shape[2]
     hid = head_w1.shape[1]
     rays = depth_target.shape[0]
+    groups = nb * cells // 256
     chunks = (-(-27 * ch // 128) + 1) * (ch // 8)
-    assert chunks <= count and cap & (cap - 1) == 0 and cells == 512 and rays % 128 == 0
+    assert chunks <= count and cap & (cap - 1) == 0 and cap >= 256 and cells == 512 and rays % 128 == 0
     operands = (
         bricks[0],
         conv_w,
@@ -573,39 +587,27 @@
         in_specs=[vmem] * len(operands),
         out_specs=(vmem, vmem, vmem),
         scratch_shapes=[
-            pltpu.VMEM((ch, 27 * ch), BF16),
-            pltpu.VMEM((hid, ch), BF16),
-            pltpu.VMEM((ch, 3 * hid), BF16),
             pltpu.VMEM((SAMP, rays), jnp.int32),
-            pltpu.VMEM((n, 1, cap), jnp.int32),
-            pltpu.VMEM((n, 1, cap), jnp.int32),
-            pltpu.VMEM((nb * ch, cells), BF16),
-            pltpu.VMEM((nb * ch, cells), F32),
-            pltpu.VMEM((nb, 27 * ch, cells), BF16),
-            pltpu.VMEM((nb, 27 * ch, cells), BF16),
-            pltpu.VMEM((n, cells, cap), BF16),
-            pltpu.VMEM((SAMP, cap, rays), BF16),
-            pltpu.VMEM((n, ch, cap), BF16),
-            pltpu.VMEM((n, ch, cap), BF16),
-            pltpu.VMEM((n, hid, cap), F32),
-            pltpu.VMEM((n, hid, cap), F32),
-            pltpu.VMEM((n, cap), F32),
-            pltpu.VMEM((n, cap), F32),
-            pltpu.VMEM((n, cap), F32),
-            pltpu.VMEM((n, cap), F32),
+            pltpu.VMEM((nb, ch, cells), BF16),
+            pltpu.VMEM((nb, ch, cells), F32),
+            pltpu.VMEM((nb, 9 * ch, cells), BF16),
+            pltpu.VMEM((nb, 9 * ch, cells), BF16),
+            pltpu.VMEM((nb, ch, cells), BF16),
+            pltpu.VMEM((SAMP, 256, rays), BF16),
+            pltpu.VMEM((nb, hid, cells), F32),
+            pltpu.VMEM((nb, hid, cells), F32),
+            pltpu.VMEM((2 * groups, 256), F32),
+            pltpu.VMEM((n, 2 * groups, 256), F32),
             pltpu.VMEM((shells, 8, rays), F32),
-            pltpu.VMEM((n, ch, cap), F32),
-            pltpu.VMEM((n, ch, cap), F32),
-            pltpu.VMEM((nb * ch, cells), F32),
+            pltpu.VMEM((n, 2 * groups, 256), F32),
+            pltpu.VMEM((n, 2 * groups, 256), F32),
             pltpu.VMEM((count, 8, 128), F32),
             pltpu.VMEM((count, 8, 128), F32),
-            dma((2, n)),
             dma((2, n)),
             dma((2, shells)),
             dma((2, n)),
             dma((2, count)),
             dma((2, count)),
-            dma,
         ],
         compiler_params=pltpu.CompilerParams(
             collective_id=0, has_side_effects=True, vmem_limit_bytes=56 * 1024 * 1024

time: 66.7 us -> 43.4 us (0.65)
  Pallas kernels: 65.9 us -> 42.6 us
    pallas_call x1, Pallas kernels: 64.1 us -> 40.8 us  [local(): pl.pallas_call(functools.partial(body, shells, n), out_shape=(jax.ShapeDt...]
where the time goes in v2:
time: 43.4 us; the launch traced here: 43.2 us
  Pallas kernels  42.6 us (98%)
  between operations  0.65 us (1%)
    pallas_call x1, Pallas kernels, local(): pl.pallas_call(functools.partial(body, shells, n), out_shape=(jax.ShapeDt...  40.8 us
    pallas_call x1, Pallas kernels, local(): pl.pallas_call(functools.partial(finish, 1.0 / (rays * n)), out_shape=(ja...  1.82 us

profile of v2, /device:TPU:0, one launch (start us, length us, event | category | flops | bytes accessed | tf_op | source)
XLA Modules:
  0.0 43.2 jit_solution(8075014872275190700)
XLA Ops:
  0.6 40.8 %shard_map.170 = (bf16[8,32,512]{2,1,0:T(8,128)(2,1)}, f32[1,512]{1,0:T(1,128)}, f32[32,8,128]{2,1,0:T(8,128)}) custom-call(bf16[8,32,512]{2,1,0:T(8,128)(2,1)} %bitcast.14, bf16[32,864]{1,0:T(8,128)(2,1)} %conv_w.1, f32[1,32]{1,0:T(1,128)} %bitcast.20, bf16[32,64]{1,0:T(8,128)(2,1)} %w1.1, f32[1,64]{1,0:T(1,128)} %bitcast.21, f32[2,64]{1,0:T(2,128)} %bitcast.19, ...), custom_call_target="tpu_custom_call" | custom-call | tf_op jit(solution)/shard_map/pallas_call | solution.py:580
  41.4 1.8 %shard_map.171 = (f32[1,1]{1,0:T(1,128)}, f32[32,864]{1,0:T(8,128)}, f32[1,32]{1,0:T(1,128)}, f32[32,64]{1,0:T(8,128)}, f32[1,64]{1,0:T(1,128)}, /*index=5*/f32[...) custom-call(f32[32,8,128]{2,1,0:T(8,128)} %get-tuple-element.19.reduced, ...), custom_call_target="tpu_custom_call" | custom-call | tf_op jit(solution)/shard_map/pallas_call | solution.py:616

commit v3 on v2

--- a/solution.py
+++ b/solution.py
@@ -127,14 +127,15 @@
     lane = lax.broadcasted_iota(jnp.int32, (1, cells), 1)
     plane = lane >> 6
 
+    shell_after = [shell] + [lax.rem(shell + k, shells) for k in range(1, shells)]
+    sector_after = [sector] + [lax.rem(sector + k, n) for k in range(1, n)]
+
     def flat_peer(k):
-        peer = lax.rem(me + k, count)
-        return peer, {"shell": lax.div(peer, n), "sector": lax.rem(peer, n)}
+        to_shell, to_sector = shell_after[k // n], sector_after[k % n]
+        return to_shell * n + to_sector, {"shell": to_shell, "sector": to_sector}
 
     barrier = pltpu.get_barrier_semaphore()
-
-    @pl.loop(1, count)
-    def _(k):
+    for k in range(1, count):
         _, where = flat_peer(k)
         pl.semaphore_signal(barrier, inc=1, device_id=where, device_id_type=MESH)
 
@@ -143,21 +144,10 @@
     w2_density = column(w2[0:1, :])
     w2_intensity = column(w2[1:2, :])
     w1_t = matmul_nt(repeated_eye(hid, 1), w1[...]).astype(BF16)
-    w1_rep = matmul(w1[...], repeated_eye(hid, 3)).astype(BF16)
     wide_w = conv_w[...].astype(F32)
     width = 9 * ch
     conv_rows = jnp.concatenate(
         [wide_w[:, a * width : (a + 1) * width] for a in range(3)], axis=0
-    ).astype(BF16)
-    turned = jnp.transpose(wide_w)
-    back_rows = jnp.concatenate(
-        [
-            jnp.concatenate(
-                [turned[(9 * a + 8 - k) * ch : (9 * a + 9 - k) * ch] for k in range(9)], axis=1
-            )
-            for a in range(3)
-        ],
-        axis=0,
     ).astype(BF16)
     block = SAMP * 128
     ray_of = lax.broadcasted_iota(jnp.int32, (block, 128), 0) // SAMP
@@ -209,7 +199,7 @@
             dst_ref=tables.at[sector],
             send_sem=table_sems.at[0, k],
             recv_sem=table_sems.at[1, k],
-            device_id={"shell": shell, "sector": lax.rem(sector + k, n)},
+            device_id={"shell": shell, "sector": sector_after[k]},
             device_id_type=MESH,
         )
 
@@ -284,7 +274,7 @@
             dst_ref=shell_buf.at[shell],
             send_sem=shell_sems.at[0, k],
             recv_sem=shell_sems.at[1, k],
-            device_id={"shell": lax.rem(shell + k, shells), "sector": sector},
+            device_id={"shell": shell_after[k], "sector": sector},
             device_id_type=MESH,
         )
 
@@ -361,7 +351,7 @@
     cell_send[...] = table_grad.reshape(n, 2 * groups, 256)
 
     def give_back(k):
-        peer = lax.rem(sector + k, n)
+        peer = sector_after[k]
         return pltpu.make_async_remote_copy(
             src_ref=cell_send.at[peer],
             dst_ref=cell_recv.at[sector],
@@ -374,6 +364,17 @@
     for k in range(1, n):
         give_back(k).start()
     cell_recv[sector] = cell_send[sector]
+    w1_rep = matmul(w1[...], repeated_eye(hid, 3)).astype(BF16)
+    turned = jnp.transpose(wide_w)
+    back_rows = jnp.concatenate(
+        [
+            jnp.concatenate(
+                [turned[(9 * a + 8 - k) * ch : (9 * a + 9 - k) * ch] for k in range(9)], axis=1
+            )
+            for a in range(3)
+        ],
+        axis=0,
+    ).astype(BF16)
     for k in range(1, n):
         give_back(k).wait()
     table_grad = jnp.sum(cell_recv[...], axis=0)
@@ -457,8 +458,7 @@
             device_id_type=MESH,
         )
 
-    @pl.loop(1, count)
-    def _(k):
+    for k in range(1, count):
         to_reducer(k).start()
 
     red_recv[me] = pack[me]
@@ -474,21 +474,18 @@
     for b in range(nb // 2):
         brick_back(b)
 
-    @pl.loop(1, count)
-    def _(k):
+    for k in range(1, count):
         to_reducer(k).wait()
 
     reduced[me] = jnp.sum(red_recv[...], axis=0)
 
-    @pl.loop(1, count)
-    def _(k):
+    for k in range(1, count):
         to_everyone(k).start()
 
     for b in range(nb // 2, nb):
         brick_back(b)
 
-    @pl.loop(1, count)
-    def _(k):
+    for k in range(1, count):
         to_everyone(k).wait()
 
 

time: 43.4 us -> 44 us (1.014)
  Pallas kernels: 42.6 us -> 43.2 us
    pallas_call x1, Pallas kernels: 40.8 us -> 41.4 us  [local(): pl.pallas_call(functools.partial(body, shells, n), out_shape=(jax.ShapeDt...]
where the time goes in v3:
time: 44 us; the launch traced here: 43.8 us
  Pallas kernels  43.2 us (98%)
  between operations  0.65 us (1%)
    pallas_call x1, Pallas kernels, local(): pl.pallas_call(functools.partial(body, shells, n), out_shape=(jax.ShapeDt...  41.4 us
    pallas_call x1, Pallas kernels, local(): pl.pallas_call(functools.partial(finish, 1.0 / (rays * n)), out_shape=(ja...  1.82 us

profile of v3, /device:TPU:0, one launch (start us, length us, event | category | flops | bytes accessed | tf_op | source)
XLA Modules:
  0.0 43.8 jit_solution(17231798671519800685)
XLA Ops:
  0.6 41.4 %shard_map.170 = (bf16[8,32,512]{2,1,0:T(8,128)(2,1)}, f32[1,512]{1,0:T(1,128)}, f32[32,8,128]{2,1,0:T(8,128)}) custom-call(bf16[8,32,512]{2,1,0:T(8,128)(2,1)} %bitcast.14, bf16[32,864]{1,0:T(8,128)(2,1)} %conv_w.1, f32[1,32]{1,0:T(1,128)} %bitcast.20, bf16[32,64]{1,0:T(8,128)(2,1)} %w1.1, f32[1,64]{1,0:T(1,128)} %bitcast.21, f32[2,64]{1,0:T(2,128)} %bitcast.19, ...), custom_call_target="tpu_custom_call" | custom-call | tf_op jit(solution)/shard_map/pallas_call | solution.py:577
  42.0 1.8 %shard_map.171 = (f32[1,1]{1,0:T(1,128)}, f32[32,864]{1,0:T(8,128)}, f32[1,32]{1,0:T(1,128)}, f32[32,64]{1,0:T(8,128)}, f32[1,64]{1,0:T(1,128)}, /*index=5*/f32[...) custom-call(f32[32,8,128]{2,1,0:T(8,128)} %get-tuple-element.19.reduced, ...), custom_call_target="tpu_custom_call" | custom-call | tf_op jit(solution)/shard_map/pallas_call | solution.py:613

commit v4 on v3

--- a/solution.py
+++ b/solution.py
@@ -230,14 +230,13 @@
         give_table(k).wait()
 
     everything = tables[...].reshape(n * 2 * groups, 256)
-    everything = jnp.concatenate([p.astype(BF16) for p in split(everything, 2)], axis=0)
+    everything = jnp.concatenate([p.astype(BF16) for p in split(everything, 2)], axis=1)
     group_of = lax.broadcasted_iota(jnp.int32, (groups, rays), 0)
     total = n * 2 * groups
     dens = []
     inten = []
     for k in range(SAMP):
-        got = matmul(everything, hot[k])
-        got = got[:total] + got[total:]
+        got = matmul(everything, jnp.concatenate([hot[k], hot[k]], axis=0))
         sums = [jnp.zeros((groups, rays), F32)] * 2
         for w in range(n):
             mine = group_of == codes[k] - w * groups

time: 44 us -> 44.2 us (level)
  no operation moved by 1% of the time
where the time goes in v4:
time: 44.2 us; the launch traced here: 44.1 us
  Pallas kernels  43.4 us (98%)
  between operations  0.65 us (1%)
    pallas_call x1, Pallas kernels, local(): pl.pallas_call(functools.partial(body, shells, n), out_shape=(jax.ShapeDt...  41.6 us
    pallas_call x1, Pallas kernels, local(): pl.pallas_call(functools.partial(finish, 1.0 / (rays * n)), out_shape=(ja...  1.82 us

profile of v4, /device:TPU:0, one launch (start us, length us, event | category | flops | bytes accessed | tf_op | source)
XLA Modules:
  0.0 44.1 jit_solution(10377259048839874273)
XLA Ops:
  0.6 41.6 %shard_map.170 = (bf16[8,32,512]{2,1,0:T(8,128)(2,1)}, f32[1,512]{1,0:T(1,128)}, f32[32,8,128]{2,1,0:T(8,128)}) custom-call(bf16[8,32,512]{2,1,0:T(8,128)(2,1)} %bitcast.14, bf16[32,864]{1,0:T(8,128)(2,1)} %conv_w.1, f32[1,32]{1,0:T(1,128)} %bitcast.20, bf16[32,64]{1,0:T(8,128)(2,1)} %w1.1, f32[1,64]{1,0:T(1,128)} %bitcast.21, f32[2,64]{1,0:T(2,128)} %bitcast.19, ...), custom_call_target="tpu_custom_call" | custom-call | tf_op jit(solution)/shard_map/pallas_call | solution.py:576
  42.3 1.8 %shard_map.171 = (f32[1,1]{1,0:T(1,128)}, f32[32,864]{1,0:T(8,128)}, f32[1,32]{1,0:T(1,128)}, f32[32,64]{1,0:T(8,128)}, f32[1,64]{1,0:T(1,128)}, /*index=5*/f32[...) custom-call(f32[32,8,128]{2,1,0:T(8,128)} %get-tuple-element.19.reduced, ...), custom_call_target="tpu_custom_call" | custom-call | tf_op jit(solution)/shard_map/pallas_call | solution.py:612
